TPU v7x, 32 devices: a whole 2x2x4 slice. The times are simulated.
32 devices in a mesh: grp: 2 (over y), row: 4 (over z), col: 2 (over x), sub: 2 (over core).
Axes of the slice: x: 2, y: 2, z: 4, core: 2. Of those that a mesh axis runs over, the one named last changes fastest.
Arguments:
- filament_slot: int32 [16384], P(('grp', 'row', 'col', 'sub')), parts along dimension 0, may hold values from 0 to 8191, each once
- wire_radius: float32 [16384], P(('grp', 'row', 'col', 'sub')), parts along dimension 0, may hold values from 0.02 to 0.05
- strand_radius: float32 [128], P('grp'), parts along dimension 0, may hold values from 0.2 to 1
- test_matrix: float32 [64, 16384], P(None, ('grp', 'row', 'col', 'sub')), parts along dimension 1, may hold values from -6 to 6
Outputs:
- ortho_basis: float32 [64, 16384], P(None, ('grp', 'row', 'col', 'sub')), parts along dimension 1
- sketch_factor: float32 [128, 64], P('grp'), parts along dimension 0
There are 2 independent parts, one for each index of `grp`. A program takes and returns all parts, laid end to end along the dimension named above; each array names one. Nothing has to cross between parts.
Inputs may be any that keep to these rules, and one draw needn't show every extreme that they name: `filament_slot`: every number from 0 to 8191 occurs exactly once.
All inputs are finite; a program needn't handle non-finite values.
Results may differ from a plain program's by a relative error of at most 0.0005.
Values sent between devices are 32-bit elements; how exact they have to be, the bound alone decides.
A program may use at most 64 MiB of HBM per device.

v0:
```python
import math
import jax
import jax.numpy as jnp
from jax import lax
from jax.sharding import PartitionSpec as P

SEGMENTS = 128
mu_scale = 1e-05
twist_rate = 4.0 * math.pi


def from_behind(shard, axis, by):
    count = lax.axis_size(axis)
    return lax.ppermute(shard, axis, [(i, (i + by) % count) for i in range(count)])


def filament_geometry(filament_slot, wire_radius, strand_radius):
    strand = filament_slot // SEGMENTS
    segment = filament_slot % SEGMENTS
    strand_count = strand_radius.shape[0]
    onehot = (strand[None, :] == jnp.arange(strand_count, dtype=jnp.int32)[:, None]).astype(
        jnp.float32
    )
    radius = jnp.sum(onehot * strand_radius[:, None], axis=0)
    phase = 2.0 * math.pi / strand_count * strand.astype(jnp.float32)
    height = (segment.astype(jnp.float32) + 0.5) / SEGMENTS
    twist_angle = phase + twist_rate * height
    cosine_part = jnp.cos(twist_angle)
    sine_part = jnp.sin(twist_angle)
    return jnp.stack(
        [
            radius * cosine_part,
            radius * sine_part,
            height,
            -twist_rate * radius * sine_part,
            twist_rate * radius * cosine_part,
            jnp.ones_like(height),
            wire_radius * wire_radius,
        ]
    )


def source_block(targets, sources, columns):
    delta_x = sources[0][:, None] - targets[0][None, :]
    delta_y = sources[1][:, None] - targets[1][None, :]
    delta_z = sources[2][:, None] - targets[2][None, :]
    distance = (
        delta_x * delta_x
        + delta_y * delta_y
        + delta_z * delta_z
        + sources[6][:, None]
        + targets[6][None, :]
    )
    alignment = (
        sources[3][:, None] * targets[3][None, :]
        + sources[4][:, None] * targets[4][None, :]
        + sources[5][:, None] * targets[5][None, :]
    )
    kernel = mu_scale * alignment * lax.rsqrt(distance)
    return jnp.dot(
        columns, kernel, precision=lax.Precision.HIGHEST, preferred_element_type=jnp.float32
    )


def sweep_sources(targets, sources, columns):
    source_count = sources.shape[1]
    block_len = math.gcd(source_count, 2048)
    block_count = source_count // block_len
    if block_count == 1:
        return source_block(targets, sources, columns)

    def add_block(block_index, running):
        offset = block_index * block_len
        geo_part = lax.dynamic_slice_in_dim(sources, offset, block_len, 1)
        col_part = lax.dynamic_slice_in_dim(columns, offset, block_len, 1)
        return running + source_block(targets, geo_part, col_part)

    initial = jnp.zeros((columns.shape[0], targets.shape[1]), jnp.float32)
    return lax.fori_loop(0, block_count, add_block, initial)


def per_device(filament_slot, wire_radius, strand_radius, test_matrix):
    targets = filament_geometry(filament_slot, wire_radius, strand_radius)
    geo_row, col_row = (
        lax.all_gather(targets, ("col", "sub"), axis=1, tiled=True),
        lax.all_gather(test_matrix, ("col", "sub"), axis=1, tiled=True),
    )
    sketch = sweep_sources(targets, geo_row, col_row)
    half_cycle = lax.axis_size("row") // 2

    def both_ways(turn_index, state_now):
        running, ahead_geo, ahead_cols, behind_geo, behind_cols = state_now
        ahead_geo, ahead_cols = from_behind((ahead_geo, ahead_cols), "row", 1)
        behind_geo, behind_cols = from_behind((behind_geo, behind_cols), "row", -1)
        running = running + sweep_sources(targets, ahead_geo, ahead_cols)
        running = running + sweep_sources(targets, behind_geo, behind_cols)
        return (running, ahead_geo, ahead_cols, behind_geo, behind_cols)

    state_end = lax.fori_loop(
        1, half_cycle, both_ways, (sketch, geo_row, col_row, geo_row, col_row)
    )
    far_geo, far_cols = from_behind((state_end[1], state_end[2]), "row", 1)
    sketch = state_end[0] + sweep_sources(targets, far_geo, far_cols)
    local_gram = jnp.dot(
        sketch, sketch.T, precision=lax.Precision.HIGHEST, preferred_element_type=jnp.float32
    )
    gram_matrix = lax.psum(local_gram, ("row", "col", "sub"))
    cholesky_low = jnp.linalg.cholesky(gram_matrix)
    solved = jax.scipy.linalg.solve_triangular(cholesky_low, sketch, lower=True)
    filament_total = (
        sketch.shape[1] * lax.axis_size("row") * lax.axis_size("col") * lax.axis_size("sub")
    )
    scale_root = math.sqrt(filament_total)
    return (solved * scale_root, cholesky_low.T / scale_root)


def solution(mesh):
    return jax.shard_map(
        per_device,
        mesh=mesh,
        in_specs=(
            P(("grp", "row", "col", "sub")),
            P(("grp", "row", "col", "sub")),
            P("grp"),
            P(None, ("grp", "row", "col", "sub")),
        ),
        out_specs=(P(None, ("grp", "row", "col", "sub")), P("grp", None)),
        check_vma=False,
    )
```

profile of v0, /device:TPU:0, one launch (start us, length us, event | category | flops | bytes accessed | tf_op | source)
XLA Modules:
  0.0 137.8 jit_solution(15863045663286231874)
XLA Ops:
  0.6 0.0 copy-start.1
  0.6 0.0 copy-start
  0.7 9.0 %all_gather.7 = f32[64,2048]{1,0:T(8,128)S(1)} all-gather(f32[64,512]{1,0:T(8,128)} %param.7), channel_id=1, replica_groups=mesh['grp'=2,'row'=4,'col'=2,'sub'=2] {'col','sub'}, dimensions={1}, use_global_device_ids=true | all-gather | bytes 655360 | tf_op jit(solution)/shard_map/all_gather | solution.py:86
  9.6 3.6 %collective-permute-start.3 = (f32[64,2048]{1,0:T(8,128)S(1)}, f32[64,2048]{1,0:T(8,128)S(1)}, u32[]{:S(2)}, u32[]{:S(2)}) collective-permute-start(f32[64,2048]{1,0:T(8,128)S(1)} %all_gather.7), channel_id=1, source_target_pairs={{0,12},{4,0},{8,4},{12,8},{1,13},{5,1},{9,5},{13,9},{2,14},{6,2},{... | collective-permute-start | bytes 1572872 | tf_op jit(solution)/shard_map/while/body/eval_jaxpr/ppermute | solution.py:14
  13.2 0.0 collective-permute-start.1
  13.2 0.1 fusion.146
  13.3 0.0 copy-done.2
  13.3 0.1 select_reduce_fusion
  13.5 5.2 %all_gather.6 = f32[7,2048]{1,0:T(8,128)S(1)} all-gather(f32[7,512]{1,0:T(8,128)S(1)} %stack.27), channel_id=1, replica_groups=mesh['grp'=2,'row'=4,'col'=2,'sub'=2] {'col','sub'}, dimensions={1}, use_global_device_ids=true | all-gather | bytes 71680 | tf_op jit(solution)/shard_map/all_gather | solution.py:85
  18.8 3.8 %collective-permute-start.2 = (f32[7,2048]{1,0:T(8,128)S(1)}, f32[7,2048]{1,0:T(8,128)S(1)}, u32[]{:S(2)}, u32[]{:S(2)}) collective-permute-start(f32[7,2048]{1,0:T(8,128)S(1)} %all_gather.6), channel_id=1, source_target_pairs={{0,12},{4,0},{8,4},{12,8},{1,13},{5,1},{9,5},{13,9},{2,14},{6,2},{... | collective-permute-start | bytes 172040 | tf_op jit(solution)/shard_map/while/body/eval_jaxpr/ppermute | solution.py:14
  22.6 0.0 collective-permute-start
  22.6 5.4 %fusion.54 = f32[512,64]{0,1:T(8,128)S(1)} fusion(f32[64,2048]{1,0:T(8,128)S(1)} %all_gather.7, f32[512]{0:T(512)S(1)} %mul.293, f32[2048]{0:T(1024)S(1)} %bitcast.74, f32[512]{0:T(512)S(1)} %get-tuple-element.81, f32[2048]{0:T(1024)S(1)} %bitcast.75, f32[512]{0:T(512)S(1)} %get-tuple-element.79, f32[2048]{0:T(1024)S(1)} %bitcast.76, ...), kind=kOutput, calls=%fused_computation.54 | convolution fusion | flops 822083584 | bytes 724992 | tf_op jit(solution)/shard_map/dot_general | solution.py:60
  28.0 11.9 %collective-permute-done = f32[7,2048]{1,0:T(8,128)S(1)} collective-permute-done((f32[7,2048]{1,0:T(8,128)S(1)}, f32[7,2048]{1,0:T(8,128)S(1)}, u32[]{:S(2)}, u32[]{:S(2)}) %collective-permute-start) | collective-permute-done | bytes 57376 | tf_op jit(solution)/shard_map/while/body/eval_jaxpr/ppermute | solution.py:14
  40.0 1.6 %collective-permute-start.4 = (f32[7,2048]{1,0:T(8,128)S(1)}, f32[7,2048]{1,0:T(8,128)S(1)}, u32[]{:S(2)}, u32[]{:S(2)}) collective-permute-start(f32[7,2048]{1,0:T(8,128)S(1)} %collective-permute-done), channel_id=1, source_target_pairs={{0,4},{4,8},{8,12},{12,0},{1,5},{5,9},{9,13},{13,1},{2,6},{6,10},{... | collective-permute-start | bytes 172040 | tf_op jit(solution)/shard_map/ppermute | solution.py:14
  41.6 0.0 collective-permute-done.2
  41.6 4.4 %collective-permute-done.4 = f32[7,2048]{1,0:T(8,128)S(1)} collective-permute-done((f32[7,2048]{1,0:T(8,128)S(1)}, f32[7,2048]{1,0:T(8,128)S(1)}, u32[]{:S(2)}, u32[]{:S(2)}) %collective-permute-start.4) | collective-permute-done | bytes 57376 | tf_op jit(solution)/shard_map/ppermute | solution.py:14
  46.1 0.0 collective-permute-done.1
  46.1 0.2 collective-permute-start.5
  46.4 0.0 collective-permute-done.3
  46.4 5.5 %fusion.18 = f32[512,64]{0,1:T(8,128)S(1)} fusion(f32[64,2048]{1,0:T(8,128)S(1)} %collective-permute-done.3, f32[2048]{0:T(1024)S(1)} %bitcast.67, f32[2048]{0:T(1024)S(1)} %bitcast.68, f32[2048]{0:T(1024)S(1)} %bitcast.69, f32[2048]{0:T(1024)S(1)} %bitcast.70, f32[2048]{0:T(1024)S(1)} %bitcast.71, f32[2048]{0:T(1024)S(1)} %bitcast.72, ...), kind=kOutput, calls=%fused_computation.18 | convolution fusion | flops 822083584 | bytes 724992 | tf_op jit(solution)/shard_map/while/body/eval_jaxpr/dot_general | solution.py:60
  51.9 5.5 %fusion.131 = f32[512,64]{0,1:T(8,128)S(1)} fusion(f32[512,64]{0,1:T(8,128)S(1)} %fusion.18, f32[512,64]{0,1:T(8,128)S(1)} %fusion.54, f32[64,2048]{1,0:T(8,128)S(1)} %collective-permute-done.1, f32[2048]{0:T(1024)S(1)} %bitcast.53, f32[2048]{0:T(1024)S(1)} %bitcast.54, f32[2048]{0:T(1024)S(1)} %bitcast.55, f32[2048]{0:T(1024)S(1)} %bitcast.56, ...), kind=kOutput, calls=%fused_computation.130 | convolution fusion | flops 822149120 | bytes 987136 | tf_op jit(solution)/shard_map/while/body/eval_jaxpr/dot_general | solution.py:60
  57.3 3.1 %collective-permute-done.5 = f32[64,2048]{1,0:T(8,128)S(1)} collective-permute-done((f32[64,2048]{1,0:T(8,128)S(1)}, f32[64,2048]{1,0:T(8,128)S(1)}, u32[]{:S(2)}, u32[]{:S(2)}) %collective-permute-start.5) | collective-permute-done | bytes 524320 | tf_op jit(solution)/shard_map/ppermute | solution.py:14
  60.4 5.7 %fusion.134 = f32[512,64]{0,1:T(8,128)S(1)} fusion(f32[512,64]{0,1:T(8,128)S(1)} %fusion.131, f32[64,2048]{1,0:T(8,128)S(1)} %collective-permute-done.5, f32[2048]{0:T(1024)S(1)} %bitcast.60, f32[2048]{0:T(1024)S(1)} %bitcast.61, f32[2048]{0:T(1024)S(1)} %bitcast.62, f32[2048]{0:T(1024)S(1)} %bitcast.63, f32[2048]{0:T(1024)S(1)} %bitcast.64, ...), kind=kOutput, calls=%fused_computation.131 | convolution fusion | flops 822116352 | bytes 856064 | tf_op jit(solution)/shard_map/dot_general | solution.py:60
  66.1 0.3 fusion.151
  66.3 57.7 %psum.7 = f32[64,64]{0,1:T(8,128)S(1)} all-reduce(f32[64,64]{0,1:T(8,128)S(1)} %fusion.151), channel_id=1, replica_groups=mesh['grp'=2,'row'=4,'col'=2,'sub'=2] {'row','col','sub'}, use_global_device_ids=true, to_apply=%region_1.2 | all-reduce | flops 4096 | bytes 32768 | tf_op jit(solution)/shard_map/psum | solution.py:107
  124.0 0.1 copy.10
  124.1 5.8 %cholesky.16 = f32[64,64]{1,0:T(8,128)S(1)} custom-call(f32[64,64]{1,0:T(8,128)S(1)} %fusion.138), custom_call_target="Cholesky" | custom-call | tf_op jit(solution)/shard_map/jit(cholesky)/cholesky | solution.py:108
  129.9 0.6 compare_reduce_fusion
  130.6 0.7 multiply_bitcast_fusion
  131.3 4.9 %custom-call.7 = f32[1,64,64]{1,2,0:T(8,128)S(1)} custom-call(f32[1,64,64]{2,1,0:T(8,128)S(1)} %get-tuple-element.74), custom_call_target="InvertDiagBlocksLowerTriangular" | custom-call | tf_op jit(solution)/shard_map/jit(_solve_triangular)/triangular_solve | solution.py:109
  136.2 1.0 convolution_multiply_fusion
  137.1 0.7 copy.11
  (13 shorter events, 0.3 us)
Async XLA Ops:
  0.6 12.6 %copy-start.1 = (s32[512]{0:T(512)S(1)}, s32[512]{0:T(512)}, u32[]{:S(2)}) copy-start(s32[512]{0:T(512)} %param.4) | copy-start | bytes 6148
  0.6 12.6 %copy-start = (f32[512]{0:T(512)S(1)}, f32[512]{0:T(512)}, u32[]{:S(2)}) copy-start(f32[512]{0:T(512)} %param.5) | copy-start | bytes 6148
  0.7 12.7 %copy-start.2 = (f32[64]{0:T(128)S(1)}, f32[64]{0:T(128)}, u32[]{:S(2)}) copy-start(f32[64]{0:T(128)} %param.6) | copy-start | bytes 772
  9.6 36.8 %collective-permute-start.3 = (f32[64,2048]{1,0:T(8,128)S(1)}, f32[64,2048]{1,0:T(8,128)S(1)}, u32[]{:S(2)}, u32[]{:S(2)}) collective-permute-start(f32[64,2048]{1,0:T(8,128)S(1)} %all_gather.7), channel_id=1, source_target_pairs={{0,12},{4,0},{8,4},{12,8},{1,13},{5,1},{9,5},{13,9},{2,14},{6,2},{... | collective-permute-start | bytes 1572872 | tf_op jit(solution)/shard_map/while/body/eval_jaxpr/ppermute | solution.py:14
  13.2 32.9 %collective-permute-start.1 = (f32[64,2048]{1,0:T(8,128)S(1)}, f32[64,2048]{1,0:T(8,128)S(1)}, u32[]{:S(2)}, u32[]{:S(2)}) collective-permute-start(f32[64,2048]{1,0:T(8,128)S(1)} %all_gather.7), channel_id=1, source_target_pairs={{0,4},{4,8},{8,12},{12,0},{1,5},{5,9},{9,13},{13,1},{2,6},{6,10},{... | collective-permute-start | bytes 1572872 | tf_op jit(solution)/shard_map/while/body/eval_jaxpr/ppermute | solution.py:14
  18.8 22.8 %collective-permute-start.2 = (f32[7,2048]{1,0:T(8,128)S(1)}, f32[7,2048]{1,0:T(8,128)S(1)}, u32[]{:S(2)}, u32[]{:S(2)}) collective-permute-start(f32[7,2048]{1,0:T(8,128)S(1)} %all_gather.6), channel_id=1, source_target_pairs={{0,12},{4,0},{8,4},{12,8},{1,13},{5,1},{9,5},{13,9},{2,14},{6,2},{... | collective-permute-start | bytes 172040 | tf_op jit(solution)/shard_map/while/body/eval_jaxpr/ppermute | solution.py:14
  22.6 17.3 %collective-permute-start = (f32[7,2048]{1,0:T(8,128)S(1)}, f32[7,2048]{1,0:T(8,128)S(1)}, u32[]{:S(2)}, u32[]{:S(2)}) collective-permute-start(f32[7,2048]{1,0:T(8,128)S(1)} %all_gather.6), channel_id=1, source_target_pairs={{0,4},{4,8},{8,12},{12,0},{1,5},{5,9},{9,13},{13,1},{2,6},{6,10},{... | collective-permute-start | bytes 172040 | tf_op jit(solution)/shard_map/while/body/eval_jaxpr/ppermute | solution.py:14
  40.0 6.1 %collective-permute-start.4 = (f32[7,2048]{1,0:T(8,128)S(1)}, f32[7,2048]{1,0:T(8,128)S(1)}, u32[]{:S(2)}, u32[]{:S(2)}) collective-permute-start(f32[7,2048]{1,0:T(8,128)S(1)} %collective-permute-done), channel_id=1, source_target_pairs={{0,4},{4,8},{8,12},{12,0},{1,5},{5,9},{9,13},{13,1},{2,6},{6,10},{... | collective-permute-start | bytes 172040 | tf_op jit(solution)/shard_map/ppermute | solution.py:14
  46.1 14.3 %collective-permute-start.5 = (f32[64,2048]{1,0:T(8,128)S(1)}, f32[64,2048]{1,0:T(8,128)S(1)}, u32[]{:S(2)}, u32[]{:S(2)}) collective-permute-start(f32[64,2048]{1,0:T(8,128)S(1)} %collective-permute-done.1), channel_id=1, source_target_pairs={{0,4},{4,8},{8,12},{12,0},{1,5},{5,9},{9,13},{13,1},{2,6},{6,10},{... | collective-permute-start | bytes 1572872 | tf_op jit(solution)/shard_map/ppermute | solution.py:14
where the time goes:
time: 138 us
  blocking collectives  71.9 us (52%)
  matrix products  23.2 us (17%)
  waiting for transfers between devices  19.4 us (14%)
  other arithmetic  12.3 us (9%)
  starting transfers between devices  9.3 us (7%)
    psum x1, blocking collectives, per_device(): gram_matrix = lax.psum(local_gram, ('row', 'col', 'sub'))  57.7 us
    dot_general x4, matrix products, source_block(): jnp.dot(columns, kernel, precision=lax.Precision.HIGHEST, preferred_eleme...  22 us
    ppermute x6, waiting for transfers between devices, from_behind(): lax.ppermute(shard, axis, [(i, (i + by) % count) for i in range(count)])  19.4 us
    ppermute x6, starting transfers between devices, from_behind(): lax.ppermute(shard, axis, [(i, (i + by) % count) for i in range(count)])  9.3 us
    all_gather x1, blocking collectives, per_device(): lax.all_gather(test_matrix, ('col', 'sub'), axis=1, tiled=True)  8.96 us
    another operation x3, other arithmetic, per_device(): cholesky_low = jnp.linalg.cholesky(gram_matrix)  6.52 us
    all_gather x1, blocking collectives, per_device(): lax.all_gather(targets, ('col', 'sub'), axis=1, tiled=True)  5.25 us
    another operation x1, other arithmetic, per_device(): solved = jax.scipy.linalg.solve_triangular(cholesky_low, sketch, lower=True)  4.9 us
  transfers between devices with their start and end apart: 6, of which 3 were waited for; matrix products, arithmetic and copies ran while one was open for 12% of the time, Pallas kernels for 0%

commit v1 on v0

--- a/solution.py
+++ b/solution.py
@@ -104,7 +104,9 @@
     local_gram = jnp.dot(
         sketch, sketch.T, precision=lax.Precision.HIGHEST, preferred_element_type=jnp.float32
     )
-    gram_matrix = lax.psum(local_gram, ("row", "col", "sub"))
+    gram_matrix = local_gram
+    for name in (("col", "sub"), "row"):
+        gram_matrix = lax.psum(gram_matrix, name)
     cholesky_low = jnp.linalg.cholesky(gram_matrix)
     solved = jax.scipy.linalg.solve_triangular(cholesky_low, sketch, lower=True)
     filament_total = (

time: 138 us -> 107 us (0.78)
  blocking collectives: 71.9 us -> 40.9 us
    psum x1 -> x2, blocking collectives: 57.7 us -> 26.7 us  [per_device(): gram_matrix = lax.psum(gram_matrix, name)]
  transfers between devices with their start and end apart: 6 -> 6, of which waited for: 3 -> 3; matrix products, arithmetic and copies ran while one was open for 12% -> 16% of each run, Pallas kernels for 0% -> 0%
where the time goes in v1:
time: 107 us
  blocking collectives  40.9 us (38%)
  matrix products  23.2 us (22%)
  waiting for transfers between devices  19.4 us (18%)
  other arithmetic  12.3 us (11%)
  starting transfers between devices  9.3 us (9%)
    psum x2, blocking collectives, per_device(): gram_matrix = lax.psum(gram_matrix, name)  26.7 us
    dot_general x4, matrix products, source_block(): jnp.dot(columns, kernel, precision=lax.Precision.HIGHEST, preferred_eleme...  22 us
    ppermute x6, waiting for transfers between devices, from_behind(): lax.ppermute(shard, axis, [(i, (i + by) % count) for i in range(count)])  19.4 us
    ppermute x6, starting transfers between devices, from_behind(): lax.ppermute(shard, axis, [(i, (i + by) % count) for i in range(count)])  9.3 us
    all_gather x1, blocking collectives, per_device(): lax.all_gather(test_matrix, ('col', 'sub'), axis=1, tiled=True)  8.96 us
    another operation x3, other arithmetic, per_device(): cholesky_low = jnp.linalg.cholesky(gram_matrix)  6.52 us
    all_gather x1, blocking collectives, per_device(): lax.all_gather(targets, ('col', 'sub'), axis=1, tiled=True)  5.25 us
    another operation x1, other arithmetic, per_device(): solved = jax.scipy.linalg.solve_triangular(cholesky_low, sketch, lower=True)  4.9 us
  transfers between devices with their start and end apart: 6, of which 3 were waited for; matrix products, arithmetic and copies ran while one was open for 16% of the time, Pallas kernels for 0%

profile of v1, /device:TPU:0, one launch (start us, length us, event | category | flops | bytes accessed | tf_op | source)
XLA Modules:
  0.0 106.9 jit_solution(14736986049422566341)
XLA Ops:
  0.6 0.0 copy-start.1
  0.7 9.0 %all_gather.7 = f32[64,2048]{1,0:T(8,128)S(1)} all-gather(f32[64,512]{1,0:T(8,128)} %param.7), channel_id=1, replica_groups=mesh['grp'=2,'row'=4,'col'=2,'sub'=2] {'col','sub'}, dimensions={1}, use_global_device_ids=true | all-gather | bytes 655360 | tf_op jit(solution)/shard_map/all_gather | solution.py:86
  9.6 3.6 %collective-permute-start.3 = (f32[64,2048]{1,0:T(8,128)S(1)}, f32[64,2048]{1,0:T(8,128)S(1)}, u32[]{:S(2)}, u32[]{:S(2)}) collective-permute-start(f32[64,2048]{1,0:T(8,128)S(1)} %all_gather.7), channel_id=1, source_target_pairs={{0,12},{4,0},{8,4},{12,8},{1,13},{5,1},{9,5},{13,9},{2,14},{6,2},{... | collective-permute-start | bytes 1572872 | tf_op jit(solution)/shard_map/while/body/eval_jaxpr/ppermute | solution.py:14
  13.2 0.0 collective-permute-start.1
  13.2 0.1 fusion.146
  13.3 0.0 copy-done.2
  13.3 0.1 select_reduce_fusion
  13.5 5.2 %all_gather.6 = f32[7,2048]{1,0:T(8,128)S(1)} all-gather(f32[7,512]{1,0:T(8,128)S(1)} %stack.27), channel_id=1, replica_groups=mesh['grp'=2,'row'=4,'col'=2,'sub'=2] {'col','sub'}, dimensions={1}, use_global_device_ids=true | all-gather | bytes 71680 | tf_op jit(solution)/shard_map/all_gather | solution.py:85
  18.8 3.8 %collective-permute-start.2 = (f32[7,2048]{1,0:T(8,128)S(1)}, f32[7,2048]{1,0:T(8,128)S(1)}, u32[]{:S(2)}, u32[]{:S(2)}) collective-permute-start(f32[7,2048]{1,0:T(8,128)S(1)} %all_gather.6), channel_id=1, source_target_pairs={{0,12},{4,0},{8,4},{12,8},{1,13},{5,1},{9,5},{13,9},{2,14},{6,2},{... | collective-permute-start | bytes 172040 | tf_op jit(solution)/shard_map/while/body/eval_jaxpr/ppermute | solution.py:14
  22.6 0.0 collective-permute-start
  22.6 5.4 %fusion.54 = f32[512,64]{0,1:T(8,128)S(1)} fusion(f32[64,2048]{1,0:T(8,128)S(1)} %all_gather.7, f32[512]{0:T(512)S(1)} %mul.293, f32[2048]{0:T(1024)S(1)} %bitcast.74, f32[512]{0:T(512)S(1)} %get-tuple-element.81, f32[2048]{0:T(1024)S(1)} %bitcast.75, f32[512]{0:T(512)S(1)} %get-tuple-element.79, f32[2048]{0:T(1024)S(1)} %bitcast.76, ...), kind=kOutput, calls=%fused_computation.54 | convolution fusion | flops 822083584 | bytes 724992 | tf_op jit(solution)/shard_map/dot_general | solution.py:60
  28.0 11.9 %collective-permute-done = f32[7,2048]{1,0:T(8,128)S(1)} collective-permute-done((f32[7,2048]{1,0:T(8,128)S(1)}, f32[7,2048]{1,0:T(8,128)S(1)}, u32[]{:S(2)}, u32[]{:S(2)}) %collective-permute-start) | collective-permute-done | bytes 57376 | tf_op jit(solution)/shard_map/while/body/eval_jaxpr/ppermute | solution.py:14
  40.0 1.6 %collective-permute-start.4 = (f32[7,2048]{1,0:T(8,128)S(1)}, f32[7,2048]{1,0:T(8,128)S(1)}, u32[]{:S(2)}, u32[]{:S(2)}) collective-permute-start(f32[7,2048]{1,0:T(8,128)S(1)} %collective-permute-done), channel_id=1, source_target_pairs={{0,4},{4,8},{8,12},{12,0},{1,5},{5,9},{9,13},{13,1},{2,6},{6,10},{... | collective-permute-start | bytes 172040 | tf_op jit(solution)/shard_map/ppermute | solution.py:14
  41.6 0.0 collective-permute-done.2
  41.6 4.4 %collective-permute-done.4 = f32[7,2048]{1,0:T(8,128)S(1)} collective-permute-done((f32[7,2048]{1,0:T(8,128)S(1)}, f32[7,2048]{1,0:T(8,128)S(1)}, u32[]{:S(2)}, u32[]{:S(2)}) %collective-permute-start.4) | collective-permute-done | bytes 57376 | tf_op jit(solution)/shard_map/ppermute | solution.py:14
  46.1 0.0 collective-permute-done.1
  46.1 0.2 collective-permute-start.5
  46.4 0.0 collective-permute-done.3
  46.4 5.5 %fusion.18 = f32[512,64]{0,1:T(8,128)S(1)} fusion(f32[64,2048]{1,0:T(8,128)S(1)} %collective-permute-done.3, f32[2048]{0:T(1024)S(1)} %bitcast.67, f32[2048]{0:T(1024)S(1)} %bitcast.68, f32[2048]{0:T(1024)S(1)} %bitcast.69, f32[2048]{0:T(1024)S(1)} %bitcast.70, f32[2048]{0:T(1024)S(1)} %bitcast.71, f32[2048]{0:T(1024)S(1)} %bitcast.72, ...), kind=kOutput, calls=%fused_computation.18 | convolution fusion | flops 822083584 | bytes 724992 | tf_op jit(solution)/shard_map/while/body/eval_jaxpr/dot_general | solution.py:60
  51.9 5.5 %fusion.131 = f32[512,64]{0,1:T(8,128)S(1)} fusion(f32[512,64]{0,1:T(8,128)S(1)} %fusion.18, f32[512,64]{0,1:T(8,128)S(1)} %fusion.54, f32[64,2048]{1,0:T(8,128)S(1)} %collective-permute-done.1, f32[2048]{0:T(1024)S(1)} %bitcast.53, f32[2048]{0:T(1024)S(1)} %bitcast.54, f32[2048]{0:T(1024)S(1)} %bitcast.55, f32[2048]{0:T(1024)S(1)} %bitcast.56, ...), kind=kOutput, calls=%fused_computation.130 | convolution fusion | flops 822149120 | bytes 987136 | tf_op jit(solution)/shard_map/while/body/eval_jaxpr/dot_general | solution.py:60
  57.3 3.1 %collective-permute-done.5 = f32[64,2048]{1,0:T(8,128)S(1)} collective-permute-done((f32[64,2048]{1,0:T(8,128)S(1)}, f32[64,2048]{1,0:T(8,128)S(1)}, u32[]{:S(2)}, u32[]{:S(2)}) %collective-permute-start.5) | collective-permute-done | bytes 524320 | tf_op jit(solution)/shard_map/ppermute | solution.py:14
  60.4 5.7 %fusion.134 = f32[512,64]{0,1:T(8,128)S(1)} fusion(f32[512,64]{0,1:T(8,128)S(1)} %fusion.131, f32[64,2048]{1,0:T(8,128)S(1)} %collective-permute-done.5, f32[2048]{0:T(1024)S(1)} %bitcast.60, f32[2048]{0:T(1024)S(1)} %bitcast.61, f32[2048]{0:T(1024)S(1)} %bitcast.62, f32[2048]{0:T(1024)S(1)} %bitcast.63, f32[2048]{0:T(1024)S(1)} %bitcast.64, ...), kind=kOutput, calls=%fused_computation.131 | convolution fusion | flops 822116352 | bytes 856064 | tf_op jit(solution)/shard_map/dot_general | solution.py:60
  66.1 0.3 fusion.151
  66.3 10.3 %psum.14 = f32[64,64]{0,1:T(8,128)S(1)} all-reduce(f32[64,64]{0,1:T(8,128)S(1)} %fusion.151), channel_id=1, replica_groups=mesh['grp'=2,'row'=4,'col'=2,'sub'=2] {'col','sub'}, use_global_device_ids=true, to_apply=%region_1.2 | all-reduce | flops 4096 | bytes 32768 | tf_op jit(solution)/shard_map/psum | solution.py:109
  76.6 16.5 %psum.15 = f32[64,64]{0,1:T(8,128)S(1)} all-reduce(f32[64,64]{0,1:T(8,128)S(1)} %psum.14), channel_id=1, replica_groups=mesh['grp'=2,'row'=4,'col'=2,'sub'=2] {'row'}, use_global_device_ids=true, to_apply=%region_2.3 | all-reduce | flops 4096 | bytes 32768 | tf_op jit(solution)/shard_map/psum | solution.py:109
  93.1 0.1 copy.10
  93.2 5.8 %cholesky.16 = f32[64,64]{1,0:T(8,128)S(1)} custom-call(f32[64,64]{1,0:T(8,128)S(1)} %fusion.138), custom_call_target="Cholesky" | custom-call | tf_op jit(solution)/shard_map/jit(cholesky)/cholesky | solution.py:110
  99.1 0.6 compare_reduce_fusion
  99.7 0.7 multiply_bitcast_fusion
  100.4 4.9 %custom-call.7 = f32[1,64,64]{1,2,0:T(8,128)S(1)} custom-call(f32[1,64,64]{2,1,0:T(8,128)S(1)} %get-tuple-element.74), custom_call_target="InvertDiagBlocksLowerTriangular" | custom-call | tf_op jit(solution)/shard_map/jit(_solve_triangular)/triangular_solve | solution.py:111
  105.3 1.0 convolution_multiply_fusion
  106.2 0.7 copy.11
  (14 shorter events, 0.3 us)
Async XLA Ops:
  0.6 12.6 %copy-start.1 = (s32[512]{0:T(512)S(1)}, s32[512]{0:T(512)}, u32[]{:S(2)}) copy-start(s32[512]{0:T(512)} %param.4) | copy-start | bytes 6148
  0.6 12.6 %copy-start = (f32[512]{0:T(512)S(1)}, f32[512]{0:T(512)}, u32[]{:S(2)}) copy-start(f32[512]{0:T(512)} %param.5) | copy-start | bytes 6148
  0.7 12.7 %copy-start.2 = (f32[64]{0:T(128)S(1)}, f32[64]{0:T(128)}, u32[]{:S(2)}) copy-start(f32[64]{0:T(128)} %param.6) | copy-start | bytes 772
  9.6 36.8 %collective-permute-start.3 = (f32[64,2048]{1,0:T(8,128)S(1)}, f32[64,2048]{1,0:T(8,128)S(1)}, u32[]{:S(2)}, u32[]{:S(2)}) collective-permute-start(f32[64,2048]{1,0:T(8,128)S(1)} %all_gather.7), channel_id=1, source_target_pairs={{0,12},{4,0},{8,4},{12,8},{1,13},{5,1},{9,5},{13,9},{2,14},{6,2},{... | collective-permute-start | bytes 1572872 | tf_op jit(solution)/shard_map/while/body/eval_jaxpr/ppermute | solution.py:14
  13.2 32.9 %collective-permute-start.1 = (f32[64,2048]{1,0:T(8,128)S(1)}, f32[64,2048]{1,0:T(8,128)S(1)}, u32[]{:S(2)}, u32[]{:S(2)}) collective-permute-start(f32[64,2048]{1,0:T(8,128)S(1)} %all_gather.7), channel_id=1, source_target_pairs={{0,4},{4,8},{8,12},{12,0},{1,5},{5,9},{9,13},{13,1},{2,6},{6,10},{... | collective-permute-start | bytes 1572872 | tf_op jit(solution)/shard_map/while/body/eval_jaxpr/ppermute | solution.py:14
  18.8 22.8 %collective-permute-start.2 = (f32[7,2048]{1,0:T(8,128)S(1)}, f32[7,2048]{1,0:T(8,128)S(1)}, u32[]{:S(2)}, u32[]{:S(2)}) collective-permute-start(f32[7,2048]{1,0:T(8,128)S(1)} %all_gather.6), channel_id=1, source_target_pairs={{0,12},{4,0},{8,4},{12,8},{1,13},{5,1},{9,5},{13,9},{2,14},{6,2},{... | collective-permute-start | bytes 172040 | tf_op jit(solution)/shard_map/while/body/eval_jaxpr/ppermute | solution.py:14
  22.6 17.3 %collective-permute-start = (f32[7,2048]{1,0:T(8,128)S(1)}, f32[7,2048]{1,0:T(8,128)S(1)}, u32[]{:S(2)}, u32[]{:S(2)}) collective-permute-start(f32[7,2048]{1,0:T(8,128)S(1)} %all_gather.6), channel_id=1, source_target_pairs={{0,4},{4,8},{8,12},{12,0},{1,5},{5,9},{9,13},{13,1},{2,6},{6,10},{... | collective-permute-start | bytes 172040 | tf_op jit(solution)/shard_map/while/body/eval_jaxpr/ppermute | solution.py:14
  40.0 6.1 %collective-permute-start.4 = (f32[7,2048]{1,0:T(8,128)S(1)}, f32[7,2048]{1,0:T(8,128)S(1)}, u32[]{:S(2)}, u32[]{:S(2)}) collective-permute-start(f32[7,2048]{1,0:T(8,128)S(1)} %collective-permute-done), channel_id=1, source_target_pairs={{0,4},{4,8},{8,12},{12,0},{1,5},{5,9},{9,13},{13,1},{2,6},{6,10},{... | collective-permute-start | bytes 172040 | tf_op jit(solution)/shard_map/ppermute | solution.py:14
  46.1 14.3 %collective-permute-start.5 = (f32[64,2048]{1,0:T(8,128)S(1)}, f32[64,2048]{1,0:T(8,128)S(1)}, u32[]{:S(2)}, u32[]{:S(2)}) collective-permute-start(f32[64,2048]{1,0:T(8,128)S(1)} %collective-permute-done.1), channel_id=1, source_target_pairs={{0,4},{4,8},{8,12},{12,0},{1,5},{5,9},{9,13},{13,1},{2,6},{6,10},{... | collective-permute-start | bytes 1572872 | tf_op jit(solution)/shard_map/ppermute | solution.py:14
